TPU v7x, 32 devices: a whole 2x2x4 slice. The times are simulated.
32 devices in a mesh: lat: 4 (over y, core), lon: 8 (over z, x).
Axes of the slice: x: 2, y: 2, z: 4, core: 2. Of those that a mesh axis runs over, the one named last changes fastest.
Arguments:
- adjoint_in: float32 [4, 72, 32, 1024], P(None, None, 'lat', 'lon'), may hold values from -6 to 6
- wind_u: float32 [72, 32, 1024], P(None, 'lat', 'lon'), may hold values from -0.45 to 0.45
- wind_v: float32 [72, 32, 1024], P(None, 'lat', 'lon'), may hold values from -0.45 to 0.45
- diffusion: float32 [72, 32, 1024], P(None, 'lat', 'lon'), may hold values from 0.02 to 8
- kernel_rows: bfloat16 [72, 65536], P(None, ('lat', 'lon')), may hold values from 0 to 1
- retrieval_misfit: bfloat16 [4, 65536], P(None, ('lat', 'lon')), may hold values from -6 to 6
- retrieval_columns: int32 [65536], P(('lat', 'lon')), may hold values from 0 to 8191, as said below
- retrieval_counts: int32 [32], P(('lat', 'lon')), may hold values from 512 to 2048, as said below
- station_cells: int32 [512], P(('lat', 'lon')), may hold values from 0 to 1023
- station_misfit: float32 [4, 512], P(None, ('lat', 'lon')), may hold values from -6 to 6
Outputs:
- adjoint_out: float32 [4, 72, 32, 1024], P(None, None, 'lat', 'lon')
Inputs may be any that keep to these rules, and one draw needn't show every extreme that they name: Only the first retrieval_counts slots of a device hold live retrievals; in each latitude band one device holds 2048. `retrieval_columns`: each value names a tile of the holding device's latitude band (value // 1024) and a cell of it (row times 128 plus column). Among the live retrievals of one device at most 512 name one tile, and in each band one tile is named by exactly 512 live retrievals of every device of the band.
All inputs are finite; a program needn't handle non-finite values.
Results may differ from a plain program's by a relative error of at most 0.0003.
Values may be sent and summed in bfloat16 or wider, within the bound.
A program may use at most 128 MiB of HBM per device.

v0:
```python
import functools

import jax
import jax.numpy as jnp
from jax import lax
from jax.experimental import pallas as pl
from jax.experimental.pallas import tpu as pltpu
from jax.sharding import PartitionSpec as P

MESH = pl.DeviceIdType.MESH
F32 = jnp.float32
BF16 = jnp.bfloat16
UNROLL = 8
PARTS = 3
NT = (((1,), (1,)), ((), ()))


def route_kernel(n_lon, cap, cols, lon_cells, count_ref, rows_ref, misfit_ref, column_ref, out_ref, pay_ref):
    levels, slots = rows_ref.shape
    tracers = misfit_ref.shape[0]
    width = out_ref.shape[2]
    column = column_ref[...]
    tile = column // cols
    cell = column - tile * cols
    lat_row = cell // lon_cells
    lane = cell - lat_row * lon_cells
    slot = lax.broadcasted_iota(jnp.int32, (1, slots), 1)
    live = slot < count_ref[0]
    tile = jnp.where(live, tile, -1)
    which = lax.broadcasted_iota(jnp.int32, (n_lon, slots), 0)
    hits = jnp.where(which == tile, 1.0, 0.0).astype(F32)
    step = 256
    before = (
        lax.broadcasted_iota(jnp.int32, (step, step), 0)
        < lax.broadcasted_iota(jnp.int32, (step, step), 1)
    )
    upper = jnp.where(before, 1.0, 0.0).astype(BF16)
    base = jnp.zeros((n_lon, 1), F32)
    codes = []
    for start in range(0, slots, step):
        part = hits[:, start : start + step]
        ahead = jnp.dot(part.astype(BF16), upper, preferred_element_type=F32) + base
        codes.append(jnp.sum(part * ahead, axis=0, keepdims=True))
        base = base + jnp.sum(part, axis=1, keepdims=True)
    rank = jnp.concatenate(codes, axis=1)
    place = jnp.where(live, tile.astype(F32) * cap + rank, -1.0)
    wide = rows_ref[...].astype(F32)
    pay_ref[0 : levels - 8, :] = wide[: levels - 8].astype(BF16)
    tail = jnp.concatenate(
        [
            misfit_ref[...].astype(F32),
            lat_row.astype(F32),
            lane.astype(F32),
            jnp.zeros((8 - tracers - 2, slots), F32),
        ],
        axis=0,
    )
    pay_ref[levels - 8 : levels + 8, :] = jnp.concatenate([wide[levels - 8 :], tail], axis=0).astype(BF16)
    index = lax.broadcasted_iota(jnp.int32, (width, slots), 0).astype(F32).astype(BF16)
    one = jnp.ones((width, slots), BF16)
    none = jnp.zeros((width, slots), BF16)

    def block(j, carry):
        local = jnp.clip(place - (j * width).astype(F32), -1.0, float(width))
        spread = jnp.broadcast_to(local.astype(BF16), (width, slots))
        pick = jnp.where(spread == index, one, none)
        out_ref[j] = lax.dot_general(
            pay_ref[...], pick, NT, preferred_element_type=F32
        ).astype(BF16)
        return carry

    lax.fori_loop(0, out_ref.shape[0], block, 0)


def transport_kernel(
    n_lat, n_lon,
    adj_ref, u_ref, v_ref, k_ref, packed_ref, cell_ref, misfit_ref,
    out_ref,
    field, y_buf, kpad, fac, acc, recv,
    row_out, row_in, col_out, col_in,
    route_send, route_recv, halo_send, halo_recv,
):
    tracers, levels = adj_ref.shape[:2]
    blocks = levels // UNROLL
    per_part = blocks // PARTS
    a = lax.axis_index("lat")
    b = lax.axis_index("lon")
    north, south = lax.rem(a + 1, n_lat), lax.rem(a + n_lat - 1, n_lat)
    east, west = lax.rem(b + 1, n_lon), lax.rem(b + n_lon - 1, n_lon)
    has_north, has_south = a < n_lat - 1, a > 0
    chunk = recv.shape[1]

    barrier = pltpu.get_barrier_semaphore()
    for other in (north, south):
        pl.semaphore_signal(barrier, inc=1, device_id=(other, b), device_id_type=MESH)

    def greet(o, carry):
        pl.semaphore_signal(
            barrier, inc=1, device_id=(a, lax.rem(b + o, n_lon)), device_id_type=MESH
        )
        return carry

    lax.fori_loop(1, n_lon, greet, 0)
    pl.semaphore_wait(barrier, n_lon + 1)

    def route_copy(o):
        target = lax.rem(b + o, n_lon)
        return pltpu.make_async_remote_copy(
            src_ref=packed_ref.at[target],
            dst_ref=recv.at[o],
            send_sem=route_send.at[o],
            recv_sem=route_recv.at[o],
            device_id=(a, target),
            device_id_type=MESH,
        )

    def row_copy(step, part, side):
        return pltpu.make_async_remote_copy(
            src_ref=row_out.at[step, side, pl.ds(part * per_part, per_part)],
            dst_ref=row_in.at[step, side, pl.ds(part * per_part, per_part)],
            send_sem=halo_send.at[step, part, side],
            recv_sem=halo_recv.at[step, part, side],
            device_id=(south if side == 0 else north, b),
            device_id_type=MESH,
        )

    def col_copy(step, part, side):
        return pltpu.make_async_remote_copy(
            src_ref=col_out.at[step, side, pl.ds(part * per_part, per_part)],
            dst_ref=col_in.at[step, side, pl.ds(part * per_part, per_part)],
            send_sem=halo_send.at[step, part, 2 + side],
            recv_sem=halo_recv.at[step, part, 2 + side],
            device_id=(a, west if side == 0 else east),
            device_id_type=MESH,
        )

    def send_part(step, part):
        for side in range(2):
            col_copy(step, part, side).start()

        @pl.when(has_south)
        def _():
            row_copy(step, part, 0).start()

        @pl.when(has_north)
        def _():
            row_copy(step, part, 1).start()

    def wait_part(step, part):
        for side in range(2):
            col_copy(step, part, side).wait_recv()

        @pl.when(has_north)
        def _():
            row_copy(step, part, 0).wait_recv()

        @pl.when(has_south)
        def _():
            row_copy(step, part, 1).wait_recv()

    def wait_sent(step, part):
        for side in range(2):
            col_copy(step, part, side).wait_send()

        @pl.when(has_south)
        def _():
            row_copy(step, part, 0).wait_send()

        @pl.when(has_north)
        def _():
            row_copy(step, part, 1).wait_send()

    lanes = lax.broadcasted_iota(jnp.int32, (8, 128), 1)
    subs = lax.broadcasted_iota(jnp.int32, (8, 128), 0)
    zero = jnp.zeros((8, 128), F32)
    first_lane, last_lane = lanes == 0, lanes == 127
    first_sub, last_sub = subs == 0, subs == 7

    def keep_edges(step, block, slot, x, packs):
        row_out[step, 0, block, slot : slot + 1, :] = x[0:1]
        row_out[step, 1, block, slot : slot + 1, :] = x[7:8]
        here = lanes == slot
        return (
            jnp.where(here, jnp.broadcast_to(x[:, 0:1], (8, 128)), packs[0]),
            jnp.where(here, jnp.broadcast_to(x[:, 127:128], (8, 128)), packs[1]),
        )

    def put_packs(step, block, packs):
        col_out[step, 0, block] = packs[0]
        col_out[step, 1, block] = packs[1]

    def over_parts(step, body, carry, wait, send):
        def part_body(part, carry):
            if wait is not None:
                wait_part(wait, part)
            carry = lax.fori_loop(
                part * per_part, (part + 1) * per_part, body, carry
            )
            if send is not None:
                send_part(send, part)
            return carry

        return lax.fori_loop(0, PARTS, part_body, carry)

    def level_at(ascending, block, i):
        count = block * UNROLL + i
        return count if ascending else levels - 1 - count

    for t in range(tracers):
        spot = subs * 128 + lanes
        add = zero
        for s in range(cell_ref.shape[0]):
            add = add + jnp.where(spot == cell_ref[s], misfit_ref[t, s], 0.0)
        field[0, t] = adj_ref[t, 0] + add
    kpad[0] = zero

    def start_body(block, carry):
        packs = (zero, zero)
        for i in range(UNROLL):
            level = block * UNROLL + i
            kpad[level + 1] = k_ref[level]
            for t in range(tracers):
                x = adj_ref[t, level]
                x = jnp.where(level == 0, field[0, t], x)
                field[level, t] = x
                packs = keep_edges(0, block, i * tracers + t, x, packs)
        put_packs(0, block, packs)
        return carry

    over_parts(0, start_body, 0, None, 0)

    def route_start(o, carry):
        route_copy(o).start()
        return carry

    lax.fori_loop(1, n_lon, route_start, 0)

    def factor_body(block, carry):
        for i in range(UNROLL):
            new = []
            for d in range(2):
                level = level_at(d == 0, block, i)
                below, above = kpad[level], kpad[level + 1]
                back, ahead = (below, above) if d == 0 else (above, below)
                inverse = 1.0 / (1.0 + below + above - back * back * carry[d])
                fac[d, 0, level] = inverse
                fac[d, 1, level] = back * inverse
                fac[d, 2, level] = ahead * inverse
                new.append(inverse)
            carry = tuple(new)
        return carry

    lax.fori_loop(0, blocks, factor_body, (zero, zero))

    def advance(step, ascending, emit, send):
        d = 0 if ascending else 1

        def sweep(block, carry):
            ys = list(carry)
            col_e, col_w = col_in[step, 0, block], col_in[step, 1, block]
            for i in range(UNROLL):
                level = level_at(ascending, block, i)
                u, v = u_ref[level], v_ref[level]
                inverse, back = fac[d, 0, level], fac[d, 1, level]
                up, vp = jnp.maximum(u, 0.0), jnp.maximum(v, 0.0)
                un, vn = jnp.maximum(-u, 0.0), jnp.maximum(-v, 0.0)
                own = 1.0 - (up + un) - (vp + vn)
                for t in range(tracers):
                    slot = i * tracers + t
                    c = field[level, t]
                    e = jnp.where(first_lane, pltpu.roll(col_e, (128 - slot) % 128, 1), c)
                    e = pltpu.roll(e, 127, 1)
                    w = jnp.where(last_lane, pltpu.roll(col_w, 127 - slot, 1), c)
                    w = pltpu.roll(w, 1, 1)
                    row_n = jnp.broadcast_to(row_in[step, 0, block, slot : slot + 1, :], (8, 128))
                    row_s = jnp.broadcast_to(row_in[step, 1, block, slot : slot + 1, :], (8, 128))
                    n = jnp.where(last_sub, row_n, pltpu.roll(c, 7, 0))
                    s = jnp.where(first_sub, row_s, pltpu.roll(c, 1, 0))
                    q = (own * c + up * e) + (un * w) + (vp * n + vn * s)
                    y = q * inverse + back * ys[t]
                    y_buf[level, t] = y
                    ys[t] = y
            return tuple(ys)

        over_parts(step, sweep, (zero,) * tracers, step, None)

        def substitute(block, carry):
            xs = list(carry)
            packs = (zero, zero)
            for i in range(UNROLL):
                level = level_at(not ascending, block, i)
                ahead = fac[d, 2, level]
                for t in range(tracers):
                    x = y_buf[level, t] + ahead * xs[t]
                    xs[t] = x
                    emit(level, t, x)
                    if send is not None:
                        packs = keep_edges(send, block, i * tracers + t, x, packs)
            if send is not None:
                put_packs(send, block, packs)
            return tuple(xs)

        over_parts(step, substitute, (zero,) * tracers, None, send)

    def to_field(level, t, x):
        field[level, t] = x

    def to_out(level, t, x):
        out_ref[t, level] = x

    @pl.when(jnp.logical_not(has_north))
    def _():
        for step in range(3):
            row_in[step, 0] = jnp.zeros(row_in.shape[2:], F32)

    @pl.when(jnp.logical_not(has_south))
    def _():
        for step in range(3):
            row_in[step, 1] = jnp.zeros(row_in.shape[2:], F32)

    acc[...] = jnp.zeros_like(acc)
    recv[0] = packed_ref[b]

    advance(0, True, to_field, None)

    def force(o, carry):
        @pl.when(o > 0)
        def _():
            route_copy(o).wait_recv()

        data = jnp.concatenate([recv[o, h] for h in range(chunk)], axis=1)
        height, width = data.shape
        meta = data[height - 16 :].astype(F32)
        lat_row = meta[8 + tracers : 9 + tracers]
        lane = meta[9 + tracers : 10 + tracers].astype(jnp.int32)
        spots = lax.broadcasted_iota(jnp.int32, (128, width), 0)
        hit = jnp.where(spots == lane, 1.0, 0.0).astype(BF16)
        right = jnp.concatenate(
            [hit * meta[8 + t : 9 + t].astype(BF16) for t in range(tracers)], axis=0
        )
        left = jnp.concatenate(
            [data * jnp.where(lat_row == r, 1.0, 0.0).astype(BF16) for r in range(8)], axis=0
        )
        total = lax.dot_general(left, right, NT, preferred_element_type=F32)
        for t in range(tracers):
            acc[t] += total[:, t * 128 : (t + 1) * 128]
        return carry

    lax.fori_loop(0, n_lon, force, 0)

    pitch = acc.shape[1] // 8

    def inject_body(block, carry):
        packs = (zero, zero)
        for i in range(UNROLL):
            level = level_at(False, block, i)
            for t in range(tracers):
                x = field[level, t] + acc[t, pl.ds(level, 8, pitch), :]
                field[level, t] = x
                packs = keep_edges(1, block, i * tracers + t, x, packs)
        put_packs(1, block, packs)
        return carry

    over_parts(1, inject_body, 0, None, 1)
    advance(1, False, to_field, 2)
    advance(2, True, to_out, None)

    def route_sent(o, carry):
        route_copy(o).wait_send()
        return carry

    lax.fori_loop(1, n_lon, route_sent, 0)

    def sent(part, carry):
        for step in range(3):
            wait_sent(step, part)
        return carry

    lax.fori_loop(0, PARTS, sent, 0)


def body(
    n_lat, n_lon,
    adjoint_in, wind_u, wind_v, diffusion, kernel_rows, retrieval_misfit,
    retrieval_columns, retrieval_counts, station_cells, station_misfit,
):
    tracers, levels, lat_rows, lon_cells = adjoint_in.shape
    cols = lat_rows * lon_cells
    slots = kernel_rows.shape[1]
    cap = 2 * slots // n_lon
    width = min(cap, 256)
    chunk = cap // width
    height = levels + 8
    vmem, smem = pl.BlockSpec(memory_space=pltpu.VMEM), pl.BlockSpec(memory_space=pltpu.SMEM)
    packed = pl.pallas_call(
        functools.partial(route_kernel, n_lon, cap, cols, lon_cells),
        out_shape=jax.ShapeDtypeStruct((n_lon * chunk, height, width), BF16),
        in_specs=[smem, vmem, vmem, vmem],
        out_specs=vmem,
        scratch_shapes=[pltpu.VMEM((height, slots), BF16)],
        compiler_params=pltpu.CompilerParams(vmem_limit_bytes=48 * 2**20),
        name="route",
    )(retrieval_counts, kernel_rows, retrieval_misfit, retrieval_columns.reshape(1, slots))
    packed = packed.reshape(n_lon, chunk, height, width)
    blocks = levels // UNROLL
    edge = UNROLL * tracers
    return pl.pallas_call(
        functools.partial(transport_kernel, n_lat, n_lon),
        out_shape=jax.ShapeDtypeStruct(adjoint_in.shape, F32),
        in_specs=[vmem] * 5 + [smem] * 2,
        out_specs=vmem,
        scratch_shapes=[
            pltpu.VMEM((levels, tracers, 8, 128), F32),
            pltpu.VMEM((levels, tracers, 8, 128), F32),
            pltpu.VMEM((levels + 1, 8, 128), F32),
            pltpu.VMEM((2, 3, levels, 8, 128), F32),
            pltpu.VMEM((tracers, 8 * height, 128), F32),
            pltpu.VMEM((n_lon, chunk, height, width), BF16),
            pltpu.VMEM((3, 2, blocks, edge, 128), F32),
            pltpu.VMEM((3, 2, blocks, edge, 128), F32),
            pltpu.VMEM((3, 2, blocks, 8, 128), F32),
            pltpu.VMEM((3, 2, blocks, 8, 128), F32),
            pltpu.SemaphoreType.DMA((n_lon,)),
            pltpu.SemaphoreType.DMA((n_lon,)),
            pltpu.SemaphoreType.DMA((3, PARTS, 4)),
            pltpu.SemaphoreType.DMA((3, PARTS, 4)),
        ],
        compiler_params=pltpu.CompilerParams(
            collective_id=0, has_side_effects=True, vmem_limit_bytes=56 * 2**20
        ),
        name="transport",
    )(adjoint_in, wind_u, wind_v, diffusion, packed, station_cells, station_misfit)


def solution(mesh):
    return jax.shard_map(
        functools.partial(body, mesh.shape["lat"], mesh.shape["lon"]),
        mesh=mesh,
        in_specs=(
            P(None, None, "lat", "lon"),
            P(None, "lat", "lon"),
            P(None, "lat", "lon"),
            P(None, "lat", "lon"),
            P(None, ("lat", "lon")),
            P(None, ("lat", "lon")),
            P(("lat", "lon")),
            P(("lat", "lon")),
            P(("lat", "lon")),
            P(None, ("lat", "lon")),
        ),
        out_specs=P(None, None, "lat", "lon"),
        check_vma=False,
    )
```

profile of v0, /device:TPU:1, one launch (start us, length us, event | category | flops | bytes accessed | tf_op | source)
XLA Modules:
  0.0 57.0 jit_solution(11304510143130505926)
XLA Ops:
  0.7 0.0 copy-start.1
  0.7 1.0 %copy-done.1 = bf16[72,2048]{1,0:T(8,128)(2,1)S(1)} copy-done((bf16[72,2048]{1,0:T(8,128)(2,1)S(1)}, bf16[72,2048]{1,0:T(8,128)(2,1)}, u32[]{:S(2)}) %copy-start.1) | copy-done | bytes 294936
  1.6 0.0 copy-start.2
  1.6 0.7 %copy-done.2 = bf16[4,2048]{1,0:T(4,128)(2,1)S(1)} copy-done((bf16[4,2048]{1,0:T(4,128)(2,1)S(1)}, bf16[4,2048]{1,0:T(4,128)(2,1)}, u32[]{:S(2)}) %copy-start.2) | copy-done | bytes 16408
  2.3 0.0 copy-start.3
  2.3 0.7 %copy-done.3 = s32[2048]{0:T(1024)S(1)} copy-done((s32[2048]{0:T(1024)S(1)}, s32[2048]{0:T(1024)}, u32[]{:S(2)}) %copy-start.3) | copy-done | bytes 8216
  3.0 7.5 %route.1 = bf16[16,80,256]{2,1,0:T(8,128)(2,1)S(1)} custom-call(s32[1]{0:T(128)S(6)} %copy.12.count_ref, bf16[72,2048]{1,0:T(8,128)(2,1)S(1)} %copy-done.1, bf16[4,2048]{1,0:T(4,128)(2,1)S(1)} %copy-done.2, s32[1,2048]{1,0:T(1,128)S(1)} %bitcast.3), custom_call_target="tpu_custom_call" | custom-call | tf_op jit(solution)/shard_map/route/pallas_call | solution.py:395
  10.6 0.0 copy-start
  10.6 0.8 %copy-done = bf16[16,80,256]{2,1,0:T(8,128)(2,1)} copy-done((bf16[16,80,256]{2,1,0:T(8,128)(2,1)}, bf16[16,80,256]{2,1,0:T(8,128)(2,1)S(1)}, u32[]{:S(2)}) %copy-start) | copy-done | bytes 655384
  11.4 43.2 %transport.1 = f32[4,72,8,128]{3,2,1,0:T(8,128)} custom-call(f32[4,72,8,128]{3,2,1,0:T(8,128)} %adj_ref.1, f32[72,8,128]{2,1,0:T(8,128)} %u_ref.1, f32[72,8,128]{2,1,0:T(8,128)} %v_ref.1, f32[72,8,128]{2,1,0:T(8,128)} %k_ref.1, bf16[8,2,80,256]{3,2,1,0:T(8,128)(2,1)} %bitcast.2, s32[16]{0:T(128)} %cell_ref.1, f32[4,16]{1,0:T(4,128)} %misfit_ref.3), custom_call_target="tpu_custom_call" | custom-call | tf_op jit(solution)/shard_map/transport/pallas_call | solution.py:407
  54.7 2.4 %copy.13 = f32[4,72,8,128]{3,2,1,0:T(8,128)} copy(f32[4,72,8,128]{3,2,1,0:T(8,128)} %transport.1) | data formatting | bytes 2359296
Async XLA Ops:
  0.7 1.0 %copy-start.1 = (bf16[72,2048]{1,0:T(8,128)(2,1)S(1)}, bf16[72,2048]{1,0:T(8,128)(2,1)}, u32[]{:S(2)}) copy-start(bf16[72,2048]{1,0:T(8,128)(2,1)} %rows_ref.1) | copy-start | bytes 884740
  1.6 0.7 %copy-start.2 = (bf16[4,2048]{1,0:T(4,128)(2,1)S(1)}, bf16[4,2048]{1,0:T(4,128)(2,1)}, u32[]{:S(2)}) copy-start(bf16[4,2048]{1,0:T(4,128)(2,1)} %misfit_ref.2) | copy-start | bytes 49156
  2.3 0.7 %copy-start.3 = (s32[2048]{0:T(1024)S(1)}, s32[2048]{0:T(1024)}, u32[]{:S(2)}) copy-start(s32[2048]{0:T(1024)} %param.16) | copy-start | bytes 24580
  10.6 0.8 %copy-start = (bf16[16,80,256]{2,1,0:T(8,128)(2,1)}, bf16[16,80,256]{2,1,0:T(8,128)(2,1)S(1)}, u32[]{:S(2)}) copy-start(bf16[16,80,256]{2,1,0:T(8,128)(2,1)S(1)} %route.1) | copy-start | bytes 1966084
where the time goes:
time: 57.3 us; the launch traced here: 57 us
  Pallas kernels  50.8 us (89%)
  local copies, waits for them, and re-layouts  5.56 us (10%)
  between operations  0.68 us (1%)
    pallas_call x1, Pallas kernels, body(): pl.pallas_call(functools.partial(transport_kernel, n_lat, n_lon), out_sha...  43.2 us
    pallas_call x1, Pallas kernels, body(): pl.pallas_call(functools.partial(route_kernel, n_lon, cap, cols, lon_cell...  7.54 us
    unnamed x9, local copies, waits for them, and re-layouts  5.56 us

commit v1 on v0

v1 whole, which is shorter than its diff:
```python
import functools

import jax
import jax.numpy as jnp
from jax import lax
from jax.experimental import pallas as pl
from jax.experimental.pallas import tpu as pltpu
from jax.sharding import PartitionSpec as P

MESH = pl.DeviceIdType.MESH
F32 = jnp.float32
BF16 = jnp.bfloat16
UNROLL = 8
PARTS = 3
GROUP = 16
EARLY = 2
NT = (((1,), (1,)), ((), ()))


def transport_kernel(
    n_lat, n_lon,
    adj_hbm, u_hbm, v_hbm, k_hbm, rows_ref, retrieved_ref, column_ref,
    count_ref, cell_ref, misfit_ref,
    out_hbm,
    adj_ref, u_ref, v_ref, out_ref,
    field, y_buf, kpad, fac, acc, pay, packed, recv, weights, spread,
    row_out, row_in, col_out, col_in,
    load_sem, store_sem, route_send, route_recv, halo_send, halo_recv,
):
    tracers, levels = adj_ref.shape[:2]
    slots = rows_ref.shape[1]
    blocks = levels // UNROLL
    a = lax.axis_index("lat")
    b = lax.axis_index("lon")
    north, south = lax.rem(a + 1, n_lat), lax.rem(a + n_lat - 1, n_lat)
    east, west = lax.rem(b + 1, n_lon), lax.rem(b + n_lon - 1, n_lon)
    has_north, has_south = a < n_lat - 1, a > 0
    chunk, height, width = recv.shape[1:]
    cap = chunk * width
    groups = height // GROUP

    loads = [
        pltpu.make_async_copy(adj_hbm, adj_ref, load_sem.at[0]),
        pltpu.make_async_copy(k_hbm, kpad.at[pl.ds(1, levels)], load_sem.at[1]),
        pltpu.make_async_copy(u_hbm, u_ref, load_sem.at[2]),
        pltpu.make_async_copy(v_hbm, v_ref, load_sem.at[3]),
    ]
    for load in loads:
        load.start()

    barrier = pltpu.get_barrier_semaphore()
    for other in (north, south):
        pl.semaphore_signal(barrier, inc=1, device_id=(other, b), device_id_type=MESH)

    def greet(o, carry):
        pl.semaphore_signal(
            barrier, inc=1, device_id=(a, lax.rem(b + o, n_lon)), device_id_type=MESH
        )
        return carry

    lax.fori_loop(1, n_lon, greet, 0)

    def route_copy(o, g):
        target = lax.rem(b + o, n_lon)
        rows = pl.ds(height - (g + 1) * GROUP, GROUP)
        return pltpu.make_async_remote_copy(
            src_ref=packed.at[o, :, rows],
            dst_ref=recv.at[o, :, rows],
            send_sem=route_send.at[o, g],
            recv_sem=route_recv.at[o, g],
            device_id=(a, target),
            device_id_type=MESH,
        )

    def send_group(g):
        def start(o, carry):
            route_copy(o, g).start()
            return carry

        lax.fori_loop(1, n_lon, start, 0)

    def bounds(step):
        if step == 1:
            return [0] + [(g * GROUP + GROUP - 8) // UNROLL for g in range(groups)]
        return [blocks * p // PARTS for p in range(PARTS + 1)]

    def row_copy(step, part, side):
        return pltpu.make_async_remote_copy(
            src_ref=row_out.at[step, side, pl.ds(bounds(step)[part], bounds(step)[part + 1] - bounds(step)[part])],
            dst_ref=row_in.at[step, side, pl.ds(bounds(step)[part], bounds(step)[part + 1] - bounds(step)[part])],
            send_sem=halo_send.at[step, part, side],
            recv_sem=halo_recv.at[step, part, side],
            device_id=(south if side == 0 else north, b),
            device_id_type=MESH,
        )

    def col_copy(step, part, side):
        return pltpu.make_async_remote_copy(
            src_ref=col_out.at[step, side, pl.ds(bounds(step)[part], bounds(step)[part + 1] - bounds(step)[part])],
            dst_ref=col_in.at[step, side, pl.ds(bounds(step)[part], bounds(step)[part + 1] - bounds(step)[part])],
            send_sem=halo_send.at[step, part, 2 + side],
            recv_sem=halo_recv.at[step, part, 2 + side],
            device_id=(a, west if side == 0 else east),
            device_id_type=MESH,
        )

    def send_part(step, part):
        for side in range(2):
            col_copy(step, part, side).start()

        @pl.when(has_south)
        def _():
            row_copy(step, part, 0).start()

        @pl.when(has_north)
        def _():
            row_copy(step, part, 1).start()

    def wait_part(step, part):
        for side in range(2):
            col_copy(step, part, side).wait_recv()

        @pl.when(has_north)
        def _():
            row_copy(step, part, 0).wait_recv()

        @pl.when(has_south)
        def _():
            row_copy(step, part, 1).wait_recv()

    def wait_sent(step, part):
        for side in range(2):
            col_copy(step, part, side).wait_send()

        @pl.when(has_south)
        def _():
            row_copy(step, part, 0).wait_send()

        @pl.when(has_north)
        def _():
            row_copy(step, part, 1).wait_send()

    lanes = lax.broadcasted_iota(jnp.int32, (8, 128), 1)
    subs = lax.broadcasted_iota(jnp.int32, (8, 128), 0)
    zero = jnp.zeros((8, 128), F32)
    first_lane, last_lane = lanes == 0, lanes == 127
    first_sub, last_sub = subs == 0, subs == 7

    def keep_edges(step, block, slot, x, packs):
        row_out[step, 0, block, slot : slot + 1, :] = x[0:1]
        row_out[step, 1, block, slot : slot + 1, :] = x[7:8]
        here = lanes == slot
        return (
            jnp.where(here, jnp.broadcast_to(x[:, 0:1], (8, 128)), packs[0]),
            jnp.where(here, jnp.broadcast_to(x[:, 127:128], (8, 128)), packs[1]),
        )

    def put_packs(step, block, packs):
        col_out[step, 0, block] = packs[0]
        col_out[step, 1, block] = packs[1]

    def over_parts(step, body, carry, wait, send):
        edges = bounds(step)
        for part in range(len(edges) - 1):
            if wait is not None:
                wait_part(wait, part)
            carry = lax.fori_loop(edges[part], edges[part + 1], body, carry)
            if send is not None:
                send_part(send, part)
        return carry

    def level_at(ascending, block, i):
        count = block * UNROLL + i
        return count if ascending else levels - 1 - count

    lat_rows, lon_cells = adj_ref.shape[2:]
    cols = lat_rows * lon_cells
    column = column_ref[...]
    tile = column // cols
    cell = column - tile * cols
    lat_row = cell // lon_cells
    lane = cell - lat_row * lon_cells
    live = lax.broadcasted_iota(jnp.int32, (1, slots), 1) < count_ref[0]
    offset = jnp.where(tile >= b, tile - b, tile - b + n_lon)
    offset = jnp.where(live, offset, -1)
    which = lax.broadcasted_iota(jnp.int32, (n_lon, slots), 0)
    hits = jnp.where(which == offset, 1.0, 0.0).astype(F32)
    step = 256
    before = (
        lax.broadcasted_iota(jnp.int32, (step, step), 0)
        < lax.broadcasted_iota(jnp.int32, (step, step), 1)
    )
    upper = jnp.where(before, 1.0, 0.0).astype(BF16)
    base = jnp.zeros((n_lon, 1), F32)
    ranks = []
    for start in range(0, slots, step):
        part = hits[:, start : start + step]
        ahead = jnp.dot(part.astype(BF16), upper, preferred_element_type=F32) + base
        ranks.append(jnp.sum(part * ahead, axis=0, keepdims=True))
        base = base + jnp.sum(part, axis=1, keepdims=True)
    rank = jnp.concatenate(ranks, axis=1)
    half = jnp.zeros((1, slots), F32)
    for h in range(1, chunk):
        half = half + jnp.where(rank >= float(h * width), 1.0, 0.0)
    place = jnp.where(live, offset.astype(F32) * chunk + half, -1.0)
    within = (rank - half * width).astype(BF16)
    wide = rows_ref[...].astype(F32)
    pay[0 : levels - 8, :] = wide[: levels - 8].astype(BF16)
    tail = jnp.concatenate(
        [
            retrieved_ref[...].astype(F32),
            lat_row.astype(F32),
            lane.astype(F32),
            jnp.zeros((8 - tracers - 2, slots), F32),
        ],
        axis=0,
    )
    pay[levels - 8 : levels + 8, :] = jnp.concatenate([wide[levels - 8 :], tail], axis=0).astype(BF16)
    index = lax.broadcasted_iota(jnp.int32, (width, slots), 0).astype(F32).astype(BF16)
    pick = jnp.where(
        jnp.broadcast_to(within, (width, slots)) == index,
        jnp.ones((width, slots), BF16),
        jnp.zeros((width, slots), BF16),
    )
    weights[...] = pick

    loads[0].wait()
    loads[1].wait()
    for t in range(tracers):
        spot = subs * 128 + lanes
        add = zero
        for s in range(cell_ref.shape[0]):
            add = add + jnp.where(spot == cell_ref[s], misfit_ref[t, s], 0.0)
        adj_ref[t, 0] = adj_ref[t, 0] + add
    kpad[0] = zero

    def start_body(block, carry):
        packs = (zero, zero)
        for i in range(UNROLL):
            level = block * UNROLL + i
            for t in range(tracers):
                packs = keep_edges(0, block, i * tracers + t, adj_ref[t, level], packs)
        put_packs(0, block, packs)
        return carry

    lax.fori_loop(0, blocks, start_body, 0)
    pl.semaphore_wait(barrier, n_lon + 1)
    for part in range(PARTS):
        send_part(0, part)

    several = max(1, 4 // chunk)

    def pack_body(turn, carry):
        picks = []
        for i in range(several * chunk):
            here = (turn * (several * chunk) + i).astype(F32)
            mask = jnp.where(place == here, 1.0, 0.0).astype(BF16)
            picks.append(pay[...] * mask)
        left = jnp.concatenate(picks, axis=0)
        total = lax.dot_general(left, weights[...], NT, preferred_element_type=F32).astype(BF16)
        for i in range(several):
            o = turn * several + i
            for h in range(chunk):
                at = (i * chunk + h) * height
                packed[o, h] = total[at : at + height]

            @pl.when(o > 0)
            def _():
                for g in range(EARLY):
                    route_copy(o, g).start()

        return carry

    lax.fori_loop(0, n_lon // several, pack_body, 0)
    recv[0] = packed[0]
    send_group(EARLY)

    def factor_body(block, carry):
        for i in range(UNROLL):
            new = []
            for d in range(2):
                level = level_at(d == 0, block, i)
                below, above = kpad[level], kpad[level + 1]
                back, ahead = (below, above) if d == 0 else (above, below)
                inverse = 1.0 / (1.0 + below + above - back * back * carry[d])
                fac[d, 0, level] = inverse
                fac[d, 1, level] = back * inverse
                fac[d, 2, level] = ahead * inverse
                new.append(inverse)
            carry = tuple(new)
        return carry

    lax.fori_loop(0, blocks, factor_body, (zero, zero))

    def sweep_of(step, ascending, fetch):
        d = 0 if ascending else 1

        def sweep(block, carry):
            ys = list(carry)
            col_e, col_w = col_in[step, 0, block], col_in[step, 1, block]
            for i in range(UNROLL):
                level = level_at(ascending, block, i)
                u, v = u_ref[level], v_ref[level]
                inverse, back = fac[d, 0, level], fac[d, 1, level]
                up, vp = jnp.maximum(u, 0.0), jnp.maximum(v, 0.0)
                un, vn = jnp.maximum(-u, 0.0), jnp.maximum(-v, 0.0)
                own = 1.0 - (up + un) - (vp + vn)
                for t in range(tracers):
                    slot = i * tracers + t
                    c = fetch(level, t)
                    e = jnp.where(
                        last_lane, pltpu.roll(col_e, 127 - slot, 1), pltpu.roll(c, 127, 1)
                    )
                    w = jnp.where(
                        first_lane, pltpu.roll(col_w, (128 - slot) % 128, 1), pltpu.roll(c, 1, 1)
                    )
                    row_n = jnp.broadcast_to(row_in[step, 0, block, slot : slot + 1, :], (8, 128))
                    row_s = jnp.broadcast_to(row_in[step, 1, block, slot : slot + 1, :], (8, 128))
                    n = jnp.where(last_sub, row_n, pltpu.roll(c, 7, 0))
                    s = jnp.where(first_sub, row_s, pltpu.roll(c, 1, 0))
                    q = (own * c + up * e) + (un * w) + (vp * n + vn * s)
                    y = q * inverse + back * ys[t]
                    y_buf[level, t] = y
                    ys[t] = y
            return tuple(ys)

        return sweep

    def substitute_of(step, ascending, emit, send):
        d = 0 if ascending else 1

        def substitute(block, carry):
            xs = list(carry)
            packs = (zero, zero)
            for i in range(UNROLL):
                level = level_at(not ascending, block, i)
                ahead = fac[d, 2, level]
                for t in range(tracers):
                    x = y_buf[level, t] + ahead * xs[t]
                    xs[t] = x
                    emit(level, t, x)
                    if send is not None:
                        packs = keep_edges(send, block, i * tracers + t, x, packs)
            if send is not None:
                put_packs(send, block, packs)
            return tuple(xs)

        return substitute

    def to_field(level, t, x):
        field[level, t] = x

    def to_out(level, t, x):
        out_ref[t, level] = x

    @pl.when(jnp.logical_not(has_north))
    def _():
        for step in range(3):
            row_in[step, 0] = jnp.zeros(row_in.shape[2:], F32)

    @pl.when(jnp.logical_not(has_south))
    def _():
        for step in range(3):
            row_in[step, 1] = jnp.zeros(row_in.shape[2:], F32)

    def from_field(level, t):
        return field[level, t]

    def from_input(level, t):
        return adj_ref[t, level]

    none = (zero,) * tracers
    loads[2].wait()
    loads[3].wait()
    over_parts(0, sweep_of(0, True, from_input), none, 0, None)
    send_group(EARLY + 1)
    over_parts(0, substitute_of(0, True, to_field, None), none, None, None)

    def read(o, rows):
        return jnp.concatenate([recv[o, h, rows] for h in range(chunk)], axis=1)

    def force(g, o):
        rows = pl.ds(height - (g + 1) * GROUP, GROUP)
        meta = read(o, pl.ds(height - GROUP, GROUP)).astype(F32)
        if g == 0:
            spots = lax.broadcasted_iota(jnp.int32, (128, cap), 0)
            lane_of = meta[GROUP - 7 + tracers : GROUP - 6 + tracers].astype(jnp.int32)
            hit = jnp.where(spots == lane_of, 1.0, 0.0).astype(BF16)
            for t in range(tracers):
                misfit = meta[GROUP - 8 + t : GROUP - 7 + t].astype(BF16)
                spread[o, t * 128 : (t + 1) * 128] = hit * misfit
        row_of = meta[GROUP - 8 + tracers : GROUP - 7 + tracers]
        data = read(o, rows)
        left = jnp.concatenate(
            [data * jnp.where(row_of == r, 1.0, 0.0).astype(BF16) for r in range(8)], axis=0
        )
        return lax.dot_general(left, spread[o], NT, preferred_element_type=F32)

    sweep_1 = sweep_of(1, False, from_field)
    edges = bounds(1)
    ys = none
    for g in range(groups):
        first = force(g, 0)
        for t in range(tracers):
            acc[t] = first[:, t * 128 : (t + 1) * 128]

        def force_body(o, carry, g=g):
            route_copy(o, g).wait_recv()
            total = force(g, o)
            for t in range(tracers):
                acc[t] += total[:, t * 128 : (t + 1) * 128]
            return carry

        lax.fori_loop(1, n_lon, force_body, 0)
        if EARLY + 2 + g < groups:
            send_group(EARLY + 2 + g)

        def inject_body(block, carry, g=g):
            packs = (zero, zero)
            for i in range(UNROLL):
                level = level_at(False, block, i)
                row = level - (levels + 8 - (g + 1) * GROUP)
                for t in range(tracers):
                    x = field[level, t] + acc[t, pl.ds(row, 8, GROUP), :]
                    field[level, t] = x
                    packs = keep_edges(1, block, i * tracers + t, x, packs)
            put_packs(1, block, packs)
            return carry

        lax.fori_loop(edges[g], edges[g + 1], inject_body, 0)
        send_part(1, g)
        if g > 0:
            wait_part(1, g - 1)
            ys = lax.fori_loop(edges[g - 1], edges[g], sweep_1, ys)
    wait_part(1, groups - 1)
    lax.fori_loop(edges[groups - 1], edges[groups], sweep_1, ys)
    over_parts(0, substitute_of(1, False, to_field, 2), none, None, 2)

    over_parts(2, sweep_of(2, True, from_field), none, 2, None)
    last = substitute_of(2, True, to_out, None)
    edges = bounds(2)
    stores = []
    carry = none
    for part in range(PARTS):
        carry = lax.fori_loop(edges[part], edges[part + 1], last, carry)
        some = pl.ds(levels - edges[part + 1] * UNROLL, (edges[part + 1] - edges[part]) * UNROLL)
        store = pltpu.make_async_copy(
            out_ref.at[:, some], out_hbm.at[:, some], store_sem.at[part]
        )
        store.start()
        stores.append(store)

    def route_sent(o, carry):
        for g in range(groups):
            route_copy(o, g).wait_send()
        return carry

    lax.fori_loop(1, n_lon, route_sent, 0)
    for step in range(3):
        for part in range(len(bounds(step)) - 1):
            wait_sent(step, part)
    for store in stores:
        store.wait()


def body(
    n_lat, n_lon,
    adjoint_in, wind_u, wind_v, diffusion, kernel_rows, retrieval_misfit,
    retrieval_columns, retrieval_counts, station_cells, station_misfit,
):
    tracers, levels, lat_rows, lon_cells = adjoint_in.shape
    cols = lat_rows * lon_cells
    slots = kernel_rows.shape[1]
    cap = 2 * slots // n_lon
    width = min(cap, 256)
    chunk = cap // width
    height = levels + 8
    any_space = pl.BlockSpec(memory_space=pl.ANY)
    vmem, smem = pl.BlockSpec(memory_space=pltpu.VMEM), pl.BlockSpec(memory_space=pltpu.SMEM)
    groups = height // GROUP
    blocks = levels // UNROLL
    edge = UNROLL * tracers
    return pl.pallas_call(
        functools.partial(transport_kernel, n_lat, n_lon),
        out_shape=jax.ShapeDtypeStruct(adjoint_in.shape, F32),
        in_specs=[any_space] * 4 + [vmem] * 3 + [smem] * 3,
        out_specs=any_space,
        scratch_shapes=[
            pltpu.VMEM(adjoint_in.shape, F32),
            pltpu.VMEM(wind_u.shape, F32),
            pltpu.VMEM(wind_v.shape, F32),
            pltpu.VMEM(adjoint_in.shape, F32),
            pltpu.VMEM((levels, tracers, 8, 128), F32),
            pltpu.VMEM((levels, tracers, 8, 128), F32),
            pltpu.VMEM((levels + 1, 8, 128), F32),
            pltpu.VMEM((2, 3, levels, 8, 128), F32),
            pltpu.VMEM((tracers, 8 * GROUP, 128), F32),
            pltpu.VMEM((height, slots), BF16),
            pltpu.VMEM((n_lon, chunk, height, width), BF16),
            pltpu.VMEM((n_lon, chunk, height, width), BF16),
            pltpu.VMEM((width, slots), BF16),
            pltpu.VMEM((n_lon, tracers * 128, cap), BF16),
            pltpu.VMEM((3, 2, blocks, edge, 128), F32),
            pltpu.VMEM((3, 2, blocks, edge, 128), F32),
            pltpu.VMEM((3, 2, blocks, 8, 128), F32),
            pltpu.VMEM((3, 2, blocks, 8, 128), F32),
            pltpu.SemaphoreType.DMA((4,)),
            pltpu.SemaphoreType.DMA((PARTS,)),
            pltpu.SemaphoreType.DMA((n_lon, groups)),
            pltpu.SemaphoreType.DMA((n_lon, groups)),
            pltpu.SemaphoreType.DMA((3, max(groups, PARTS), 4)),
            pltpu.SemaphoreType.DMA((3, max(groups, PARTS), 4)),
        ],
        compiler_params=pltpu.CompilerParams(
            collective_id=0, has_side_effects=True, vmem_limit_bytes=40 * 2**20
        ),
        name="transport",
    )(
        adjoint_in, wind_u, wind_v, diffusion, kernel_rows, retrieval_misfit,
        retrieval_columns.reshape(1, slots), retrieval_counts, station_cells, station_misfit,
    )


def solution(mesh):
    return jax.shard_map(
        functools.partial(body, mesh.shape["lat"], mesh.shape["lon"]),
        mesh=mesh,
        in_specs=(
            P(None, None, "lat", "lon"),
            P(None, "lat", "lon"),
            P(None, "lat", "lon"),
            P(None, "lat", "lon"),
            P(None, ("lat", "lon")),
            P(None, ("lat", "lon")),
            P(("lat", "lon")),
            P(("lat", "lon")),
            P(("lat", "lon")),
            P(None, ("lat", "lon")),
        ),
        out_specs=P(None, None, "lat", "lon"),
        check_vma=False,
    )
```

time: 57.3 us -> 57 us (level)
  Pallas kernels: 50.8 us -> 47.1 us
  local copies, waits for them, and re-layouts: 5.56 us -> 8.87 us
    pallas_call x1 -> x0, Pallas kernels: 7.54 us -> none  [body(): pl.pallas_call(functools.partial(route_kernel, n_lon, cap, cols, lon_cell...]
    pallas_call x1, Pallas kernels: 43.2 us -> 47.1 us  [body(): pl.pallas_call(functools.partial(transport_kernel, n_lat, n_lon), out_sha...]
    unnamed x9 -> x19, local copies, waits for them, and re-layouts: 5.56 us -> 8.87 us
where the time goes in v1:
time: 57 us; the launch traced here: 56.6 us
  Pallas kernels  47.1 us (83%)
  local copies, waits for them, and re-layouts  8.87 us (16%)
  between operations  0.68 us (1%)
    pallas_call x1, Pallas kernels, body(): pl.pallas_call(functools.partial(transport_kernel, n_lat, n_lon), out_sha...  47.1 us
    unnamed x19, local copies, waits for them, and re-layouts  8.87 us

profile of v1, /device:TPU:1, one launch (start us, length us, event | category | flops | bytes accessed | tf_op | source)
XLA Modules:
  0.0 56.6 jit_solution(2404020422656998244)
XLA Ops:
  0.7 0.0 copy-start
  0.7 1.3 %copy-done = f32[4,72,8,128]{3,2,1,0:T(8,128)S(1)} copy-done((f32[4,72,8,128]{3,2,1,0:T(8,128)S(1)}, f32[4,72,8,128]{3,2,1,0:T(8,128)}, u32[]{:S(2)}) %copy-start) | copy-done | bytes 1179672
  1.9 0.0 copy-start.1
  1.9 1.0 %copy-done.1 = f32[72,8,128]{2,1,0:T(8,128)S(1)} copy-done((f32[72,8,128]{2,1,0:T(8,128)S(1)}, f32[72,8,128]{2,1,0:T(8,128)}, u32[]{:S(2)}) %copy-start.1) | copy-done | bytes 294936
  2.9 0.0 copy-start.2
  2.9 1.0 %copy-done.2 = f32[72,8,128]{2,1,0:T(8,128)S(1)} copy-done((f32[72,8,128]{2,1,0:T(8,128)S(1)}, f32[72,8,128]{2,1,0:T(8,128)}, u32[]{:S(2)}) %copy-start.2) | copy-done | bytes 294936
  3.8 0.0 copy-start.3
  3.9 1.0 %copy-done.3 = f32[72,8,128]{2,1,0:T(8,128)S(1)} copy-done((f32[72,8,128]{2,1,0:T(8,128)S(1)}, f32[72,8,128]{2,1,0:T(8,128)}, u32[]{:S(2)}) %copy-start.3) | copy-done | bytes 294936
  4.8 0.0 copy-start.4
  4.8 1.0 %copy-done.4 = bf16[72,2048]{1,0:T(8,128)(2,1)S(1)} copy-done((bf16[72,2048]{1,0:T(8,128)(2,1)S(1)}, bf16[72,2048]{1,0:T(8,128)(2,1)}, u32[]{:S(2)}) %copy-start.4) | copy-done | bytes 294936
  5.8 0.0 copy-start.5
  5.8 0.7 %copy-done.5 = bf16[4,2048]{1,0:T(4,128)(2,1)S(1)} copy-done((bf16[4,2048]{1,0:T(4,128)(2,1)S(1)}, bf16[4,2048]{1,0:T(4,128)(2,1)}, u32[]{:S(2)}) %copy-start.5) | copy-done | bytes 16408
  6.5 0.0 copy-start.6
  6.5 0.7 %copy-done.6 = s32[2048]{0:T(1024)S(1)} copy-done((s32[2048]{0:T(1024)S(1)}, s32[2048]{0:T(1024)}, u32[]{:S(2)}) %copy-start.6) | copy-done | bytes 8216
  7.2 0.0 copy-start.7
  7.2 0.7 %copy-done.7 = f32[4,16]{1,0:T(4,128)S(1)} copy-done((f32[4,16]{1,0:T(4,128)S(1)}, f32[4,16]{1,0:T(4,128)}, u32[]{:S(2)}) %copy-start.7) | copy-done | bytes 280
  7.9 0.0 copy-start.8
  7.9 0.7 %copy-done.8 = s32[16]{0:T(128)S(1)} copy-done((s32[16]{0:T(128)S(1)}, s32[16]{0:T(128)}, u32[]{:S(2)}) %copy-start.8) | copy-done | bytes 88
  8.5 47.1 %transport.1 = f32[4,72,8,128]{3,2,1,0:T(8,128)S(1)} custom-call(f32[4,72,8,128]{3,2,1,0:T(8,128)S(1)} %copy-done, f32[72,8,128]{2,1,0:T(8,128)S(1)} %copy-done.1, f32[72,8,128]{2,1,0:T(8,128)S(1)} %copy-done.2, f32[72,8,128]{2,1,0:T(8,128)S(1)} %copy-done.3, bf16[72,2048]{1,0:T(8,128)(2,1)S(1)} %copy-done.4, bf16[4,2048]{1,0:T(4,128)(2,1)S(1)} %copy-done.5, ...), custom_call_target="tpu_custom_call" | custom-call | tf_op jit(solution)/shard_map/transport/pallas_call | solution.py:483
  55.6 1.0 %copy.13 = f32[4,72,8,128]{3,2,1,0:T(8,128)} copy(f32[4,72,8,128]{3,2,1,0:T(8,128)S(1)} %transport.1) | data formatting | bytes 2359296
Async XLA Ops:
  0.7 1.3 %copy-start = (f32[4,72,8,128]{3,2,1,0:T(8,128)S(1)}, f32[4,72,8,128]{3,2,1,0:T(8,128)}, u32[]{:S(2)}) copy-start(f32[4,72,8,128]{3,2,1,0:T(8,128)} %adj_hbm.1) | copy-start | bytes 3538948
  1.9 1.0 %copy-start.1 = (f32[72,8,128]{2,1,0:T(8,128)S(1)}, f32[72,8,128]{2,1,0:T(8,128)}, u32[]{:S(2)}) copy-start(f32[72,8,128]{2,1,0:T(8,128)} %u_hbm.1) | copy-start | bytes 884740
  2.9 1.0 %copy-start.2 = (f32[72,8,128]{2,1,0:T(8,128)S(1)}, f32[72,8,128]{2,1,0:T(8,128)}, u32[]{:S(2)}) copy-start(f32[72,8,128]{2,1,0:T(8,128)} %v_hbm.1) | copy-start | bytes 884740
  3.8 1.0 %copy-start.3 = (f32[72,8,128]{2,1,0:T(8,128)S(1)}, f32[72,8,128]{2,1,0:T(8,128)}, u32[]{:S(2)}) copy-start(f32[72,8,128]{2,1,0:T(8,128)} %k_hbm.1) | copy-start | bytes 884740
  4.8 1.0 %copy-start.4 = (bf16[72,2048]{1,0:T(8,128)(2,1)S(1)}, bf16[72,2048]{1,0:T(8,128)(2,1)}, u32[]{:S(2)}) copy-start(bf16[72,2048]{1,0:T(8,128)(2,1)} %rows_ref.1) | copy-start | bytes 884740
  5.8 0.7 %copy-start.5 = (bf16[4,2048]{1,0:T(4,128)(2,1)S(1)}, bf16[4,2048]{1,0:T(4,128)(2,1)}, u32[]{:S(2)}) copy-start(bf16[4,2048]{1,0:T(4,128)(2,1)} %retrieved_ref.1) | copy-start | bytes 49156
  6.5 0.7 %copy-start.6 = (s32[2048]{0:T(1024)S(1)}, s32[2048]{0:T(1024)}, u32[]{:S(2)}) copy-start(s32[2048]{0:T(1024)} %param.16) | copy-start | bytes 24580
  7.2 0.7 %copy-start.7 = (f32[4,16]{1,0:T(4,128)S(1)}, f32[4,16]{1,0:T(4,128)}, u32[]{:S(2)}) copy-start(f32[4,16]{1,0:T(4,128)} %misfit_ref.1) | copy-start | bytes 772
  7.9 0.7 %copy-start.8 = (s32[16]{0:T(128)S(1)}, s32[16]{0:T(128)}, u32[]{:S(2)}) copy-start(s32[16]{0:T(128)} %cell_ref.1) | copy-start | bytes 196

commit v2 on v1

--- a/solution.py
+++ b/solution.py
@@ -19,11 +19,11 @@
 
 def transport_kernel(
     n_lat, n_lon,
-    adj_hbm, u_hbm, v_hbm, k_hbm, rows_ref, retrieved_ref, column_ref,
-    count_ref, cell_ref, misfit_ref,
+    adj_hbm, u_hbm, v_hbm, k_hbm, rows_hbm, retrieved_hbm, column_hbm,
+    count_ref, cell_hbm, misfit_hbm,
     out_hbm,
-    adj_ref, u_ref, v_ref, out_ref,
-    field, y_buf, kpad, fac, acc, pay, packed, recv, weights, spread,
+    adj_ref, u_ref, v_ref, rows_ref, retrieved_ref, column_ref, cell_ref, misfit_ref, out_ref,
+    field, y_buf, kpad, fac, acc, pay, packed, recv, weights, spread, masks, left,
     row_out, row_in, col_out, col_in,
     load_sem, store_sem, route_send, route_recv, halo_send, halo_recv,
 ):
@@ -35,8 +35,9 @@
     north, south = lax.rem(a + 1, n_lat), lax.rem(a + n_lat - 1, n_lat)
     east, west = lax.rem(b + 1, n_lon), lax.rem(b + n_lon - 1, n_lon)
     has_north, has_south = a < n_lat - 1, a > 0
-    chunk, height, width = recv.shape[1:]
-    cap = chunk * width
+    height, cap = packed.shape[1:]
+    width = weights.shape[0]
+    chunk = cap // width
     groups = height // GROUP
 
     loads = [
@@ -44,6 +45,11 @@
         pltpu.make_async_copy(k_hbm, kpad.at[pl.ds(1, levels)], load_sem.at[1]),
         pltpu.make_async_copy(u_hbm, u_ref, load_sem.at[2]),
         pltpu.make_async_copy(v_hbm, v_ref, load_sem.at[3]),
+        pltpu.make_async_copy(rows_hbm, rows_ref, load_sem.at[4]),
+        pltpu.make_async_copy(retrieved_hbm, retrieved_ref, load_sem.at[5]),
+        pltpu.make_async_copy(column_hbm, column_ref, load_sem.at[6]),
+        pltpu.make_async_copy(cell_hbm, cell_ref, load_sem.at[7]),
+        pltpu.make_async_copy(misfit_hbm, misfit_ref, load_sem.at[8]),
     ]
     for load in loads:
         load.start()
@@ -60,12 +66,15 @@
 
     lax.fori_loop(1, n_lon, greet, 0)
 
+    def group_rows(g):
+        return pl.ds(pl.multiple_of(height - (g + 1) * GROUP, GROUP), GROUP)
+
     def route_copy(o, g):
         target = lax.rem(b + o, n_lon)
-        rows = pl.ds(height - (g + 1) * GROUP, GROUP)
+        rows = group_rows(g)
         return pltpu.make_async_remote_copy(
-            src_ref=packed.at[o, :, rows],
-            dst_ref=recv.at[o, :, rows],
+            src_ref=packed.at[o, rows],
+            dst_ref=recv.at[rows, pl.ds(pl.multiple_of(o * cap, 128), cap)],
             send_sem=route_send.at[o, g],
             recv_sem=route_recv.at[o, g],
             device_id=(a, target),
@@ -79,15 +88,16 @@
 
         lax.fori_loop(1, n_lon, start, 0)
 
-    def bounds(step):
-        if step == 1:
-            return [0] + [(g * GROUP + GROUP - 8) // UNROLL for g in range(groups)]
-        return [blocks * p // PARTS for p in range(PARTS + 1)]
+    def part_size(step):
+        return GROUP // UNROLL if step == 1 else blocks // PARTS
+
+    def place_of(step, block):
+        return block + 1 if step == 1 else block
 
     def row_copy(step, part, side):
         return pltpu.make_async_remote_copy(
-            src_ref=row_out.at[step, side, pl.ds(bounds(step)[part], bounds(step)[part + 1] - bounds(step)[part])],
-            dst_ref=row_in.at[step, side, pl.ds(bounds(step)[part], bounds(step)[part + 1] - bounds(step)[part])],
+            src_ref=row_out.at[step, side, pl.ds(part * part_size(step), part_size(step))],
+            dst_ref=row_in.at[step, side, pl.ds(part * part_size(step), part_size(step))],
             send_sem=halo_send.at[step, part, side],
             recv_sem=halo_recv.at[step, part, side],
             device_id=(south if side == 0 else north, b),
@@ -96,8 +106,8 @@
 
     def col_copy(step, part, side):
         return pltpu.make_async_remote_copy(
-            src_ref=col_out.at[step, side, pl.ds(bounds(step)[part], bounds(step)[part + 1] - bounds(step)[part])],
-            dst_ref=col_in.at[step, side, pl.ds(bounds(step)[part], bounds(step)[part + 1] - bounds(step)[part])],
+            src_ref=col_out.at[step, side, pl.ds(part * part_size(step), part_size(step))],
+            dst_ref=col_in.at[step, side, pl.ds(part * part_size(step), part_size(step))],
             send_sem=halo_send.at[step, part, 2 + side],
             recv_sem=halo_recv.at[step, part, 2 + side],
             device_id=(a, west if side == 0 else east),
@@ -147,8 +157,8 @@
     first_sub, last_sub = subs == 0, subs == 7
 
     def keep_edges(step, block, slot, x, packs):
-        row_out[step, 0, block, slot : slot + 1, :] = x[0:1]
-        row_out[step, 1, block, slot : slot + 1, :] = x[7:8]
+        row_out[step, 0, place_of(step, block), slot : slot + 1, :] = x[0:1]
+        row_out[step, 1, place_of(step, block), slot : slot + 1, :] = x[7:8]
         here = lanes == slot
         return (
             jnp.where(here, jnp.broadcast_to(x[:, 0:1], (8, 128)), packs[0]),
@@ -156,18 +166,21 @@
         )
 
     def put_packs(step, block, packs):
-        col_out[step, 0, block] = packs[0]
-        col_out[step, 1, block] = packs[1]
+        col_out[step, 0, place_of(step, block)] = packs[0]
+        col_out[step, 1, place_of(step, block)] = packs[1]
 
     def over_parts(step, body, carry, wait, send):
-        edges = bounds(step)
-        for part in range(len(edges) - 1):
+        size = part_size(step)
+
+        def part_body(part, carry):
             if wait is not None:
                 wait_part(wait, part)
-            carry = lax.fori_loop(edges[part], edges[part + 1], body, carry)
+            carry = lax.fori_loop(part * size, (part + 1) * size, body, carry)
             if send is not None:
                 send_part(send, part)
-        return carry
+            return carry
+
+        return lax.fori_loop(0, blocks // size, part_body, carry)
 
     def level_at(ascending, block, i):
         count = block * UNROLL + i
@@ -175,6 +188,7 @@
 
     lat_rows, lon_cells = adj_ref.shape[2:]
     cols = lat_rows * lon_cells
+    loads[6].wait()
     column = column_ref[...]
     tile = column // cols
     cell = column - tile * cols
@@ -204,6 +218,8 @@
         half = half + jnp.where(rank >= float(h * width), 1.0, 0.0)
     place = jnp.where(live, offset.astype(F32) * chunk + half, -1.0)
     within = (rank - half * width).astype(BF16)
+    loads[4].wait()
+    loads[5].wait()
     wide = rows_ref[...].astype(F32)
     pay[0 : levels - 8, :] = wide[: levels - 8].astype(BF16)
     tail = jnp.concatenate(
@@ -224,13 +240,16 @@
     )
     weights[...] = pick
 
-    loads[0].wait()
-    loads[1].wait()
+    for n in (0, 1, 7, 8):
+        loads[n].wait()
+    station_cell, station_misfit = cell_ref[...], misfit_ref[...]
     for t in range(tracers):
         spot = subs * 128 + lanes
         add = zero
-        for s in range(cell_ref.shape[0]):
-            add = add + jnp.where(spot == cell_ref[s], misfit_ref[t, s], 0.0)
+        for s in range(cell_ref.shape[1]):
+            at = jnp.broadcast_to(station_cell[:, s : s + 1], (8, 128))
+            term = jnp.broadcast_to(station_misfit[t : t + 1, s : s + 1], (8, 128))
+            add = add + jnp.where(spot == at, term, 0.0)
         adj_ref[t, 0] = adj_ref[t, 0] + add
     kpad[0] = zero
 
@@ -245,8 +264,15 @@
 
     lax.fori_loop(0, blocks, start_body, 0)
     pl.semaphore_wait(barrier, n_lon + 1)
-    for part in range(PARTS):
+    for side in range(2):
+        row_out[1, side, 0] = jnp.zeros(row_out.shape[3:], F32)
+        col_out[1, side, 0] = zero
+
+    def send_first(part, carry):
         send_part(0, part)
+        return carry
+
+    lax.fori_loop(0, PARTS, send_first, 0)
 
     several = max(1, 4 // chunk)
 
@@ -256,13 +282,13 @@
             here = (turn * (several * chunk) + i).astype(F32)
             mask = jnp.where(place == here, 1.0, 0.0).astype(BF16)
             picks.append(pay[...] * mask)
-        left = jnp.concatenate(picks, axis=0)
-        total = lax.dot_general(left, weights[...], NT, preferred_element_type=F32).astype(BF16)
+        stacked = jnp.concatenate(picks, axis=0)
+        total = lax.dot_general(stacked, weights[...], NT, preferred_element_type=F32).astype(BF16)
         for i in range(several):
             o = turn * several + i
             for h in range(chunk):
                 at = (i * chunk + h) * height
-                packed[o, h] = total[at : at + height]
+                packed[o, :, h * width : (h + 1) * width] = total[at : at + height]
 
             @pl.when(o > 0)
             def _():
@@ -272,7 +298,7 @@
         return carry
 
     lax.fori_loop(0, n_lon // several, pack_body, 0)
-    recv[0] = packed[0]
+    recv[:, 0:cap] = packed[0]
     send_group(EARLY)
 
     def factor_body(block, carry):
@@ -297,7 +323,8 @@
 
         def sweep(block, carry):
             ys = list(carry)
-            col_e, col_w = col_in[step, 0, block], col_in[step, 1, block]
+            spot = place_of(step, block)
+            col_e, col_w = col_in[step, 0, spot], col_in[step, 1, spot]
             for i in range(UNROLL):
                 level = level_at(ascending, block, i)
                 u, v = u_ref[level], v_ref[level]
@@ -314,8 +341,8 @@
                     w = jnp.where(
                         first_lane, pltpu.roll(col_w, (128 - slot) % 128, 1), pltpu.roll(c, 1, 1)
                     )
-                    row_n = jnp.broadcast_to(row_in[step, 0, block, slot : slot + 1, :], (8, 128))
-                    row_s = jnp.broadcast_to(row_in[step, 1, block, slot : slot + 1, :], (8, 128))
+                    row_n = jnp.broadcast_to(row_in[step, 0, spot, slot : slot + 1, :], (8, 128))
+                    row_s = jnp.broadcast_to(row_in[step, 1, spot, slot : slot + 1, :], (8, 128))
                     n = jnp.where(last_sub, row_n, pltpu.roll(c, 7, 0))
                     s = jnp.where(first_sub, row_s, pltpu.roll(c, 1, 0))
                     q = (own * c + up * e) + (un * w) + (vp * n + vn * s)
@@ -376,46 +403,52 @@
     send_group(EARLY + 1)
     over_parts(0, substitute_of(0, True, to_field, None), none, None, None)
 
-    def read(o, rows):
-        return jnp.concatenate([recv[o, h, rows] for h in range(chunk)], axis=1)
-
-    def force(g, o):
-        rows = pl.ds(height - (g + 1) * GROUP, GROUP)
-        meta = read(o, pl.ds(height - GROUP, GROUP)).astype(F32)
-        if g == 0:
-            spots = lax.broadcasted_iota(jnp.int32, (128, cap), 0)
-            lane_of = meta[GROUP - 7 + tracers : GROUP - 6 + tracers].astype(jnp.int32)
-            hit = jnp.where(spots == lane_of, 1.0, 0.0).astype(BF16)
-            for t in range(tracers):
-                misfit = meta[GROUP - 8 + t : GROUP - 7 + t].astype(BF16)
-                spread[o, t * 128 : (t + 1) * 128] = hit * misfit
+    total_slots = n_lon * cap
+    piece = min(512, total_slots)
+
+    def prepare(n, carry):
+        here = pl.ds(pl.multiple_of(n * piece, 128), piece)
+        meta = recv[height - GROUP : height, here].astype(F32)
+        spots = lax.broadcasted_iota(jnp.int32, (128, piece), 0)
+        lane_of = meta[GROUP - 7 + tracers : GROUP - 6 + tracers].astype(jnp.int32)
+        hit = jnp.where(spots == lane_of, 1.0, 0.0).astype(BF16)
+        for t in range(tracers):
+            misfit = meta[GROUP - 8 + t : GROUP - 7 + t].astype(BF16)
+            spread[t * 128 : (t + 1) * 128, here] = hit * misfit
         row_of = meta[GROUP - 8 + tracers : GROUP - 7 + tracers]
-        data = read(o, rows)
-        left = jnp.concatenate(
-            [data * jnp.where(row_of == r, 1.0, 0.0).astype(BF16) for r in range(8)], axis=0
-        )
-        return lax.dot_general(left, spread[o], NT, preferred_element_type=F32)
+        for r in range(8):
+            mask = jnp.where(row_of == r, 1.0, 0.0).astype(BF16)
+            masks[r, :, here] = jnp.broadcast_to(mask, (GROUP, piece))
+        return carry
 
     sweep_1 = sweep_of(1, False, from_field)
-    edges = bounds(1)
-    ys = none
-    for g in range(groups):
-        first = force(g, 0)
+
+    def group_edge(g):
+        return jnp.maximum(g * (GROUP // UNROLL) - 1, 0)
+
+    def group_body(g, ys):
+        def arrived(o, carry):
+            route_copy(o, g).wait_recv()
+            return carry
+
+        lax.fori_loop(1, n_lon, arrived, 0)
+
+        @pl.when(g + EARLY + 2 < groups)
+        def _():
+            send_group(g + EARLY + 2)
+
+        @pl.when(g == 0)
+        def _():
+            lax.fori_loop(0, total_slots // piece, prepare, 0)
+
+        data = recv[group_rows(g), :]
+        for r in range(8):
+            left[r * GROUP : (r + 1) * GROUP, :] = data * masks[r]
+        acc_all = lax.dot_general(left[...], spread[...], NT, preferred_element_type=F32)
         for t in range(tracers):
-            acc[t] = first[:, t * 128 : (t + 1) * 128]
-
-        def force_body(o, carry, g=g):
-            route_copy(o, g).wait_recv()
-            total = force(g, o)
-            for t in range(tracers):
-                acc[t] += total[:, t * 128 : (t + 1) * 128]
-            return carry
-
-        lax.fori_loop(1, n_lon, force_body, 0)
-        if EARLY + 2 + g < groups:
-            send_group(EARLY + 2 + g)
-
-        def inject_body(block, carry, g=g):
+            acc[t] = acc_all[:, t * 128 : (t + 1) * 128]
+
+        def inject_body(block, carry):
             packs = (zero, zero)
             for i in range(UNROLL):
                 level = level_at(False, block, i)
@@ -427,28 +460,34 @@
             put_packs(1, block, packs)
             return carry
 
-        lax.fori_loop(edges[g], edges[g + 1], inject_body, 0)
+        lax.fori_loop(group_edge(g), group_edge(g + 1), inject_body, 0)
         send_part(1, g)
-        if g > 0:
+
+        @pl.when(g > 0)
+        def _():
             wait_part(1, g - 1)
-            ys = lax.fori_loop(edges[g - 1], edges[g], sweep_1, ys)
+
+        return lax.fori_loop(group_edge(g - 1), group_edge(g), sweep_1, ys)
+
+    ys = lax.fori_loop(0, groups, group_body, none)
     wait_part(1, groups - 1)
-    lax.fori_loop(edges[groups - 1], edges[groups], sweep_1, ys)
+    lax.fori_loop(group_edge(groups - 1), group_edge(groups), sweep_1, ys)
     over_parts(0, substitute_of(1, False, to_field, 2), none, None, 2)
 
     over_parts(2, sweep_of(2, True, from_field), none, 2, None)
     last = substitute_of(2, True, to_out, None)
-    edges = bounds(2)
-    stores = []
-    carry = none
-    for part in range(PARTS):
-        carry = lax.fori_loop(edges[part], edges[part + 1], last, carry)
-        some = pl.ds(levels - edges[part + 1] * UNROLL, (edges[part + 1] - edges[part]) * UNROLL)
-        store = pltpu.make_async_copy(
-            out_ref.at[:, some], out_hbm.at[:, some], store_sem.at[part]
-        )
-        store.start()
-        stores.append(store)
+    size = part_size(2)
+
+    def store(part):
+        some = pl.ds(levels - (part + 1) * size * UNROLL, size * UNROLL)
+        return pltpu.make_async_copy(out_ref.at[:, some], out_hbm.at[:, some], store_sem.at[part])
+
+    def final(part, carry):
+        carry = lax.fori_loop(part * size, (part + 1) * size, last, carry)
+        store(part).start()
+        return carry
+
+    lax.fori_loop(0, PARTS, final, none)
 
     def route_sent(o, carry):
         for g in range(groups):
@@ -457,10 +496,18 @@
 
     lax.fori_loop(1, n_lon, route_sent, 0)
     for step in range(3):
-        for part in range(len(bounds(step)) - 1):
+
+        def sent(part, carry, step=step):
             wait_sent(step, part)
-    for store in stores:
-        store.wait()
+            return carry
+
+        lax.fori_loop(0, groups if step == 1 else PARTS, sent, 0)
+
+    def stored(part, carry):
+        store(part).wait()
+        return carry
+
+    lax.fori_loop(0, PARTS, stored, 0)
 
 
 def body(
@@ -473,22 +520,28 @@
     slots = kernel_rows.shape[1]
     cap = 2 * slots // n_lon
     width = min(cap, 256)
-    chunk = cap // width
     height = levels + 8
     any_space = pl.BlockSpec(memory_space=pl.ANY)
-    vmem, smem = pl.BlockSpec(memory_space=pltpu.VMEM), pl.BlockSpec(memory_space=pltpu.SMEM)
+    hbm = pl.BlockSpec(memory_space=pltpu.HBM)
+    stations = station_cells.shape[0]
+    smem = pl.BlockSpec(memory_space=pltpu.SMEM)
     groups = height // GROUP
     blocks = levels // UNROLL
     edge = UNROLL * tracers
     return pl.pallas_call(
         functools.partial(transport_kernel, n_lat, n_lon),
         out_shape=jax.ShapeDtypeStruct(adjoint_in.shape, F32),
-        in_specs=[any_space] * 4 + [vmem] * 3 + [smem] * 3,
+        in_specs=[hbm] * 7 + [smem] + [hbm] * 2,
         out_specs=any_space,
         scratch_shapes=[
             pltpu.VMEM(adjoint_in.shape, F32),
             pltpu.VMEM(wind_u.shape, F32),
             pltpu.VMEM(wind_v.shape, F32),
+            pltpu.VMEM(kernel_rows.shape, BF16),
+            pltpu.VMEM(retrieval_misfit.shape, BF16),
+            pltpu.VMEM((1, slots), jnp.int32),
+            pltpu.VMEM((1, stations), jnp.int32),
+            pltpu.VMEM(station_misfit.shape, F32),
             pltpu.VMEM(adjoint_in.shape, F32),
             pltpu.VMEM((levels, tracers, 8, 128), F32),
             pltpu.VMEM((levels, tracers, 8, 128), F32),
@@ -496,15 +549,17 @@
             pltpu.VMEM((2, 3, levels, 8, 128), F32),
             pltpu.VMEM((tracers, 8 * GROUP, 128), F32),
             pltpu.VMEM((height, slots), BF16),
-            pltpu.VMEM((n_lon, chunk, height, width), BF16),
-            pltpu.VMEM((n_lon, chunk, height, width), BF16),
+            pltpu.VMEM((n_lon, height, cap), BF16),
+            pltpu.VMEM((height, n_lon * cap), BF16),
             pltpu.VMEM((width, slots), BF16),
-            pltpu.VMEM((n_lon, tracers * 128, cap), BF16),
-            pltpu.VMEM((3, 2, blocks, edge, 128), F32),
-            pltpu.VMEM((3, 2, blocks, edge, 128), F32),
-            pltpu.VMEM((3, 2, blocks, 8, 128), F32),
-            pltpu.VMEM((3, 2, blocks, 8, 128), F32),
-            pltpu.SemaphoreType.DMA((4,)),
+            pltpu.VMEM((tracers * 128, n_lon * cap), BF16),
+            pltpu.VMEM((8, GROUP, n_lon * cap), BF16),
+            pltpu.VMEM((8 * GROUP, n_lon * cap), BF16),
+            pltpu.VMEM((3, 2, blocks + 1, edge, 128), F32),
+            pltpu.VMEM((3, 2, blocks + 1, edge, 128), F32),
+            pltpu.VMEM((3, 2, blocks + 1, 8, 128), F32),
+            pltpu.VMEM((3, 2, blocks + 1, 8, 128), F32),
+            pltpu.SemaphoreType.DMA((9,)),
             pltpu.SemaphoreType.DMA((PARTS,)),
             pltpu.SemaphoreType.DMA((n_lon, groups)),
             pltpu.SemaphoreType.DMA((n_lon, groups)),
@@ -517,7 +572,7 @@
         name="transport",
     )(
         adjoint_in, wind_u, wind_v, diffusion, kernel_rows, retrieval_misfit,
-        retrieval_columns.reshape(1, slots), retrieval_counts, station_cells, station_misfit,
+        retrieval_columns.reshape(1, slots), retrieval_counts, station_cells.reshape(1, stations), station_misfit,
     )
 
 

time: 57 us -> 55.3 us (0.970)
  Pallas kernels: 47.1 us -> 45.3 us
    pallas_call x1, Pallas kernels: 47.1 us -> 45.3 us  [body(): pl.pallas_call(functools.partial(transport_kernel, n_lat, n_lon), out_sha...]
where the time goes in v2:
time: 55.3 us; the launch traced here: 54.9 us
  Pallas kernels  45.3 us (82%)
  local copies, waits for them, and re-layouts  8.87 us (16%)
  between operations  0.68 us (1%)
    pallas_call x1, Pallas kernels, body(): pl.pallas_call(functools.partial(transport_kernel, n_lat, n_lon), out_sha...  45.3 us
    unnamed x19, local copies, waits for them, and re-layouts  8.87 us

profile of v2, /device:TPU:1, one launch (start us, length us, event | category | flops | bytes accessed | tf_op | source)
XLA Modules:
  0.0 54.9 jit_solution(10249796255497517326)
XLA Ops:
  0.7 0.0 copy-start
  0.7 1.3 %copy-done = f32[4,72,8,128]{3,2,1,0:T(8,128)S(1)} copy-done((f32[4,72,8,128]{3,2,1,0:T(8,128)S(1)}, f32[4,72,8,128]{3,2,1,0:T(8,128)}, u32[]{:S(2)}) %copy-start) | copy-done | bytes 1179672
  1.9 0.0 copy-start.1
  1.9 1.0 %copy-done.1 = f32[72,8,128]{2,1,0:T(8,128)S(1)} copy-done((f32[72,8,128]{2,1,0:T(8,128)S(1)}, f32[72,8,128]{2,1,0:T(8,128)}, u32[]{:S(2)}) %copy-start.1) | copy-done | bytes 294936
  2.9 0.0 copy-start.2
  2.9 1.0 %copy-done.2 = f32[72,8,128]{2,1,0:T(8,128)S(1)} copy-done((f32[72,8,128]{2,1,0:T(8,128)S(1)}, f32[72,8,128]{2,1,0:T(8,128)}, u32[]{:S(2)}) %copy-start.2) | copy-done | bytes 294936
  3.8 0.0 copy-start.3
  3.9 1.0 %copy-done.3 = f32[72,8,128]{2,1,0:T(8,128)S(1)} copy-done((f32[72,8,128]{2,1,0:T(8,128)S(1)}, f32[72,8,128]{2,1,0:T(8,128)}, u32[]{:S(2)}) %copy-start.3) | copy-done | bytes 294936
  4.8 0.0 copy-start.4
  4.8 1.0 %copy-done.4 = bf16[72,2048]{1,0:T(8,128)(2,1)S(1)} copy-done((bf16[72,2048]{1,0:T(8,128)(2,1)S(1)}, bf16[72,2048]{1,0:T(8,128)(2,1)}, u32[]{:S(2)}) %copy-start.4) | copy-done | bytes 294936
  5.8 0.0 copy-start.5
  5.8 0.7 %copy-done.5 = bf16[4,2048]{1,0:T(4,128)(2,1)S(1)} copy-done((bf16[4,2048]{1,0:T(4,128)(2,1)S(1)}, bf16[4,2048]{1,0:T(4,128)(2,1)}, u32[]{:S(2)}) %copy-start.5) | copy-done | bytes 16408
  6.5 0.0 copy-start.6
  6.5 0.7 %copy-done.6 = s32[2048]{0:T(1024)S(1)} copy-done((s32[2048]{0:T(1024)S(1)}, s32[2048]{0:T(1024)}, u32[]{:S(2)}) %copy-start.6) | copy-done | bytes 8216
  7.2 0.0 copy-start.7
  7.2 0.7 %copy-done.7 = f32[4,16]{1,0:T(4,128)S(1)} copy-done((f32[4,16]{1,0:T(4,128)S(1)}, f32[4,16]{1,0:T(4,128)}, u32[]{:S(2)}) %copy-start.7) | copy-done | bytes 280
  7.9 0.0 copy-start.8
  7.9 0.7 %copy-done.8 = s32[16]{0:T(128)S(1)} copy-done((s32[16]{0:T(128)S(1)}, s32[16]{0:T(128)}, u32[]{:S(2)}) %copy-start.8) | copy-done | bytes 88
  8.5 45.3 %transport.1 = f32[4,72,8,128]{3,2,1,0:T(8,128)S(1)} custom-call(f32[4,72,8,128]{3,2,1,0:T(8,128)S(1)} %copy-done, f32[72,8,128]{2,1,0:T(8,128)S(1)} %copy-done.1, f32[72,8,128]{2,1,0:T(8,128)S(1)} %copy-done.2, f32[72,8,128]{2,1,0:T(8,128)S(1)} %copy-done.3, bf16[72,2048]{1,0:T(8,128)(2,1)S(1)} %copy-done.4, bf16[4,2048]{1,0:T(4,128)(2,1)S(1)} %copy-done.5, ...), custom_call_target="tpu_custom_call" | custom-call | tf_op jit(solution)/shard_map/transport/pallas_call | solution.py:531
  53.9 1.0 %copy.13 = f32[4,72,8,128]{3,2,1,0:T(8,128)} copy(f32[4,72,8,128]{3,2,1,0:T(8,128)S(1)} %transport.1) | data formatting | bytes 2359296
Async XLA Ops:
  0.7 1.3 %copy-start = (f32[4,72,8,128]{3,2,1,0:T(8,128)S(1)}, f32[4,72,8,128]{3,2,1,0:T(8,128)}, u32[]{:S(2)}) copy-start(f32[4,72,8,128]{3,2,1,0:T(8,128)} %adj_hbm.1) | copy-start | bytes 3538948
  1.9 1.0 %copy-start.1 = (f32[72,8,128]{2,1,0:T(8,128)S(1)}, f32[72,8,128]{2,1,0:T(8,128)}, u32[]{:S(2)}) copy-start(f32[72,8,128]{2,1,0:T(8,128)} %u_hbm.1) | copy-start | bytes 884740
  2.9 1.0 %copy-start.2 = (f32[72,8,128]{2,1,0:T(8,128)S(1)}, f32[72,8,128]{2,1,0:T(8,128)}, u32[]{:S(2)}) copy-start(f32[72,8,128]{2,1,0:T(8,128)} %v_hbm.1) | copy-start | bytes 884740
  3.8 1.0 %copy-start.3 = (f32[72,8,128]{2,1,0:T(8,128)S(1)}, f32[72,8,128]{2,1,0:T(8,128)}, u32[]{:S(2)}) copy-start(f32[72,8,128]{2,1,0:T(8,128)} %k_hbm.1) | copy-start | bytes 884740
  4.8 1.0 %copy-start.4 = (bf16[72,2048]{1,0:T(8,128)(2,1)S(1)}, bf16[72,2048]{1,0:T(8,128)(2,1)}, u32[]{:S(2)}) copy-start(bf16[72,2048]{1,0:T(8,128)(2,1)} %rows_hbm.1) | copy-start | bytes 884740
  5.8 0.7 %copy-start.5 = (bf16[4,2048]{1,0:T(4,128)(2,1)S(1)}, bf16[4,2048]{1,0:T(4,128)(2,1)}, u32[]{:S(2)}) copy-start(bf16[4,2048]{1,0:T(4,128)(2,1)} %retrieved_hbm.1) | copy-start | bytes 49156
  6.5 0.7 %copy-start.6 = (s32[2048]{0:T(1024)S(1)}, s32[2048]{0:T(1024)}, u32[]{:S(2)}) copy-start(s32[2048]{0:T(1024)} %param.16) | copy-start | bytes 24580
  7.2 0.7 %copy-start.7 = (f32[4,16]{1,0:T(4,128)S(1)}, f32[4,16]{1,0:T(4,128)}, u32[]{:S(2)}) copy-start(f32[4,16]{1,0:T(4,128)} %misfit_hbm.1) | copy-start | bytes 772
  7.9 0.7 %copy-start.8 = (s32[16]{0:T(128)S(1)}, s32[16]{0:T(128)}, u32[]{:S(2)}) copy-start(s32[16]{0:T(128)} %param.18) | copy-start | bytes 196

commit v3 on v2

--- a/solution.py
+++ b/solution.py
@@ -14,7 +14,7 @@
 PARTS = 3
 GROUP = 16
 EARLY = 2
-NT = (((1,), (1,)), ((), ()))
+TN = (((0,), (0,)), ((), ()))
 
 
 def transport_kernel(
@@ -36,7 +36,7 @@
     east, west = lax.rem(b + 1, n_lon), lax.rem(b + n_lon - 1, n_lon)
     has_north, has_south = a < n_lat - 1, a > 0
     height, cap = packed.shape[1:]
-    width = weights.shape[0]
+    width = weights.shape[1]
     chunk = cap // width
     groups = height // GROUP
 
@@ -217,7 +217,7 @@
     for h in range(1, chunk):
         half = half + jnp.where(rank >= float(h * width), 1.0, 0.0)
     place = jnp.where(live, offset.astype(F32) * chunk + half, -1.0)
-    within = (rank - half * width).astype(BF16)
+    within = rank - half * width
     loads[4].wait()
     loads[5].wait()
     wide = rows_ref[...].astype(F32)
@@ -232,13 +232,17 @@
         axis=0,
     )
     pay[levels - 8 : levels + 8, :] = jnp.concatenate([wide[levels - 8 :], tail], axis=0).astype(BF16)
-    index = lax.broadcasted_iota(jnp.int32, (width, slots), 0).astype(F32).astype(BF16)
-    pick = jnp.where(
-        jnp.broadcast_to(within, (width, slots)) == index,
-        jnp.ones((width, slots), BF16),
-        jnp.zeros((width, slots), BF16),
-    )
-    weights[...] = pick
+    rows16 = lax.broadcasted_iota(jnp.int32, (GROUP, slots), 0)
+    column_of = jnp.where(rows16 == 0, jnp.broadcast_to(within, (GROUP, slots)), 0.0).astype(BF16)
+    spread_first = jnp.where(
+        lax.broadcasted_iota(jnp.int32, (GROUP, 128), 0) == 0, 1.0, 0.0
+    ).astype(BF16)
+    turned = lax.dot_general(column_of, spread_first, TN, preferred_element_type=F32)
+    slot_of = lax.broadcasted_iota(jnp.int32, (1, 128), 1).astype(F32)
+    for h in range(width // 128):
+        weights[:, h * 128 : (h + 1) * 128] = jnp.where(
+            turned == slot_of + float(h * 128), 1.0, 0.0
+        ).astype(BF16)
 
     for n in (0, 1, 7, 8):
         loads[n].wait()
@@ -283,7 +287,7 @@
             mask = jnp.where(place == here, 1.0, 0.0).astype(BF16)
             picks.append(pay[...] * mask)
         stacked = jnp.concatenate(picks, axis=0)
-        total = lax.dot_general(stacked, weights[...], NT, preferred_element_type=F32).astype(BF16)
+        total = jnp.dot(stacked, weights[...], preferred_element_type=F32).astype(BF16)
         for i in range(several):
             o = turn * several + i
             for h in range(chunk):
@@ -406,15 +410,22 @@
     total_slots = n_lon * cap
     piece = min(512, total_slots)
 
+    chosen_row = lax.broadcasted_iota(jnp.int32, (GROUP, (tracers + 1) * 128), 0) - (GROUP - 8)
+    chosen_block = lax.broadcasted_iota(jnp.int32, (GROUP, (tracers + 1) * 128), 1) // 128
+    wanted = jnp.where(chosen_block == tracers, tracers + 1, chosen_block)
+    chosen = jnp.where(chosen_row == wanted, 1.0, 0.0).astype(BF16)
+    lane_at = lax.broadcasted_iota(jnp.int32, (1, 128), 1).astype(F32)
+
     def prepare(n, carry):
         here = pl.ds(pl.multiple_of(n * piece, 128), piece)
-        meta = recv[height - GROUP : height, here].astype(F32)
-        spots = lax.broadcasted_iota(jnp.int32, (128, piece), 0)
-        lane_of = meta[GROUP - 7 + tracers : GROUP - 6 + tracers].astype(jnp.int32)
-        hit = jnp.where(spots == lane_of, 1.0, 0.0).astype(BF16)
+        raw = recv[height - GROUP : height, here]
+        meta = raw.astype(F32)
+        turned = lax.dot_general(raw, chosen, TN, preferred_element_type=F32)
+        hit = turned[:, tracers * 128 :] == lane_at
         for t in range(tracers):
-            misfit = meta[GROUP - 8 + t : GROUP - 7 + t].astype(BF16)
-            spread[t * 128 : (t + 1) * 128, here] = hit * misfit
+            spread[here, t * 128 : (t + 1) * 128] = jnp.where(
+                hit, turned[:, t * 128 : (t + 1) * 128], 0.0
+            ).astype(BF16)
         row_of = meta[GROUP - 8 + tracers : GROUP - 7 + tracers]
         for r in range(8):
             mask = jnp.where(row_of == r, 1.0, 0.0).astype(BF16)
@@ -444,7 +455,7 @@
         data = recv[group_rows(g), :]
         for r in range(8):
             left[r * GROUP : (r + 1) * GROUP, :] = data * masks[r]
-        acc_all = lax.dot_general(left[...], spread[...], NT, preferred_element_type=F32)
+        acc_all = jnp.dot(left[...], spread[...], preferred_element_type=F32)
         for t in range(tracers):
             acc[t] = acc_all[:, t * 128 : (t + 1) * 128]
 
@@ -551,8 +562,8 @@
             pltpu.VMEM((height, slots), BF16),
             pltpu.VMEM((n_lon, height, cap), BF16),
             pltpu.VMEM((height, n_lon * cap), BF16),
-            pltpu.VMEM((width, slots), BF16),
-            pltpu.VMEM((tracers * 128, n_lon * cap), BF16),
+            pltpu.VMEM((slots, width), BF16),
+            pltpu.VMEM((n_lon * cap, tracers * 128), BF16),
             pltpu.VMEM((8, GROUP, n_lon * cap), BF16),
             pltpu.VMEM((8 * GROUP, n_lon * cap), BF16),
             pltpu.VMEM((3, 2, blocks + 1, edge, 128), F32),
@@ -567,7 +578,7 @@
             pltpu.SemaphoreType.DMA((3, max(groups, PARTS), 4)),
         ],
         compiler_params=pltpu.CompilerParams(
-            collective_id=0, has_side_effects=True, vmem_limit_bytes=40 * 2**20
+            collective_id=0, has_side_effects=True, vmem_limit_bytes=60 * 2**20
         ),
         name="transport",
     )(

time: 55.3 us -> 48.5 us (0.88)
  local copies, waits for them, and re-layouts: 8.87 us -> 2.36 us
    unnamed x19 -> x1, local copies, waits for them, and re-layouts: 8.87 us -> 2.36 us
where the time goes in v3:
time: 48.5 us; the launch traced here: 48.3 us
  Pallas kernels  45.3 us (93%)
  local copies, waits for them, and re-layouts  2.36 us (5%)
  between operations  0.66 us (1%)
    pallas_call x1, Pallas kernels, body(): pl.pallas_call(functools.partial(transport_kernel, n_lat, n_lon), out_sha...  45.3 us
    unnamed x1, local copies, waits for them, and re-layouts  2.36 us

profile of v3, /device:TPU:1, one launch (start us, length us, event | category | flops | bytes accessed | tf_op | source)
XLA Modules:
  0.0 48.3 jit_solution(14031828481079837631)
XLA Ops:
  0.7 45.3 %transport.1 = f32[4,72,8,128]{3,2,1,0:T(8,128)} custom-call(f32[4,72,8,128]{3,2,1,0:T(8,128)} %adj_hbm.1, f32[72,8,128]{2,1,0:T(8,128)} %u_hbm.1, f32[72,8,128]{2,1,0:T(8,128)} %v_hbm.1, f32[72,8,128]{2,1,0:T(8,128)} %k_hbm.1, bf16[72,2048]{1,0:T(8,128)(2,1)} %rows_hbm.1, bf16[4,2048]{1,0:T(4,128)(2,1)} %retrieved_hbm.1, s32[1,2048]{1,0:T(1,128)} %bitcast.2, ...), custom_call_target="tpu_custom_call" | custom-call | tf_op jit(solution)/shard_map/transport/pallas_call | solution.py:542
  45.9 2.4 %copy.13 = f32[4,72,8,128]{3,2,1,0:T(8,128)} copy(f32[4,72,8,128]{3,2,1,0:T(8,128)} %transport.1) | data formatting | bytes 2359296
